TPU v7x, 32 devices: a whole 2x2x4 slice. The times are simulated.
32 devices in a mesh: dp: 8 (over y, x, core), ctx: 4 (over z).
Axes of the slice: x: 2, y: 2, z: 4, core: 2. Of those that a mesh axis runs over, the one named last changes fastest.
Arguments:
- tokens: bfloat16 [16, 1024, 2048], P('dp', 'ctx'), may hold values from -6 to 6
- cotangent: bfloat16 [16, 1024, 2048], P('dp', 'ctx'), may hold values from -6 to 6
- positions: int32 [16, 1024], P('dp', 'ctx'), may hold values from 0 to 1023, as said below
- wqkv_master: float32 [2048, 6144], P(('dp', 'ctx')), may hold values from -0.125 to 0.125
- fc1_master: float32 [2048, 8192], P(('dp', 'ctx')), may hold values from -0.125 to 0.125
- out_master: float32 [2048, 2048], P(('dp', 'ctx')), may hold values from -1.5 to 1.5
- fc2_master: float32 [2048, 8192], P(('dp', 'ctx')), may hold values from -0.0625 to 0.0625
- small_master: float32 [2048, 11], P(('dp', 'ctx')), may hold values from -0.6 to 1.3, as said below
- wqkv_first: float32 [2048, 6144], P(('dp', 'ctx')), may hold values from -128 to 128
- wqkv_second: float32 [2048, 6144], P(('dp', 'ctx')), may hold values from 1949.696 to 7815.168
- fc1_first: float32 [2048, 8192], P(('dp', 'ctx')), may hold values from -24 to 24
- fc1_second: float32 [2048, 8192], P(('dp', 'ctx')), may hold values from 78.6432 to 311.296
- out_first: float32 [2048, 2048], P(('dp', 'ctx')), may hold values from -12 to 12
- out_second: float32 [2048, 2048], P(('dp', 'ctx')), may hold values from 19.6608 to 78.6432
- fc2_first: float32 [2048, 8192], P(('dp', 'ctx')), may hold values from -56 to 56
- fc2_second: float32 [2048, 8192], P(('dp', 'ctx')), may hold values from 367.0016 to 1474.56
- small_first: float32 [2048, 11], P(('dp', 'ctx')), may hold values from -105.6 to 105.6
- small_second: float32 [2048, 11], P(('dp', 'ctx')), may hold values from 78.15168 to 21708.8
Outputs:
- mixed: bfloat16 [16, 1024, 2048], P('dp', 'ctx')
- input_grad: float32 [16, 1024, 2048], P('dp', 'ctx')
- wqkv_first_new: float32 [2048, 6144], P(('dp', 'ctx'))
- wqkv_second_new: float32 [2048, 6144], P(('dp', 'ctx'))
- wqkv_new: float32 [2048, 6144], P(('dp', 'ctx'))
- fc1_first_new: float32 [2048, 8192], P(('dp', 'ctx'))
- fc1_second_new: float32 [2048, 8192], P(('dp', 'ctx'))
- fc1_new: float32 [2048, 8192], P(('dp', 'ctx'))
- out_first_new: float32 [2048, 2048], P(('dp', 'ctx'))
- out_second_new: float32 [2048, 2048], P(('dp', 'ctx'))
- out_new: float32 [2048, 2048], P(('dp', 'ctx'))
- fc2_first_new: float32 [2048, 8192], P(('dp', 'ctx'))
- fc2_second_new: float32 [2048, 8192], P(('dp', 'ctx'))
- fc2_new: float32 [2048, 8192], P(('dp', 'ctx'))
- small_first_new: float32 [2048, 11], P(('dp', 'ctx'))
- small_second_new: float32 [2048, 11], P(('dp', 'ctx'))
- small_new: float32 [2048, 11], P(('dp', 'ctx'))
Inputs may be any that keep to these rules, and one draw needn't show every extreme that they name: In each sequence the positions rise by one from token to token, except at one token at most, where they restart at 0. `small_master`: column 0 holds gains, the others biases.
All inputs are finite; a program needn't handle non-finite values.
Results may differ from a plain program's by a relative error of at most 0.012.
The roundings to bfloat16 on the way count: a program that leaves them out, or rounds other values in their place, can miss the bound.
Values may be sent and summed in bfloat16 or wider, within the bound.
A program may use at most 640 MiB of HBM per device.

v0:
```python
import functools

import jax
import jax.numpy as jnp
from jax import lax
from jax.experimental import pallas as pl
from jax.experimental.pallas import tpu as pltpu
from jax.sharding import PartitionSpec as P

D = 2048
H = 32
HD = 64
ROT = 32
FF = 8192
STEP = 10
LANES = 128
BLOCK = 256

beta_one = 0.9
beta_two = 0.95
epsilon = 1e-08

f32 = jnp.float32
bf16 = jnp.bfloat16
EVERY = ("dp", "ctx")
GRANT = 58 * 1024 * 1024


def adamw(weight, first_old, second_old, gradient, step_rate, decay):
    first_new = beta_one * first_old + (1.0 - beta_one) * gradient
    second_new = beta_two * second_old + (1.0 - beta_two) * gradient * gradient
    first_hat = first_new / (1.0 - beta_one**STEP)
    second_hat = second_new / (1.0 - beta_two**STEP)
    weight_new = weight - step_rate * (
        first_hat / (jnp.sqrt(second_hat) + epsilon) + decay * weight
    )
    return (first_new, second_new, weight_new)


def mm(left, right, dims):
    return lax.dot_general(left, right, ((dims[:1], dims[1:]), ((), ())), preferred_element_type=f32)


def rotated(vals, cos_t, lead, trail):
    return (
        vals * cos_t + pltpu.roll(vals, LANES - 16, 1) * lead + pltpu.roll(vals, 16, 1) * trail
    )


def unrotated(vals, cos_t, lead, trail):
    return (
        vals * cos_t - pltpu.roll(vals, LANES - 16, 1) * lead - pltpu.roll(vals, 16, 1) * trail
    )


def attend_kernel(
    q_in, k_in, v_in, bias, cos_ref, lead_ref, trail_ref, q_out, k_out, v_out, o_out, log_out
):
    rows = q_in.shape[0]
    cos_t, lead, trail = cos_ref[...].T, lead_ref[...].T, trail_ref[...].T
    scale = HD ** (-0.5)
    query = rotated(q_in[...] + bias[0:1, :], cos_t, lead, trail).astype(bf16)
    key = rotated(k_in[...] + bias[1:2, :], cos_t, lead, trail).astype(bf16)
    value = (v_in[...] + bias[2:3, :]).astype(bf16)
    query = query * jnp.asarray(scale, bf16)
    q_out[...] = query
    k_out[...] = key
    v_out[...] = value
    lane = lax.broadcasted_iota(jnp.int32, (BLOCK, LANES), 1)
    on_diagonal = lax.broadcasted_iota(jnp.int32, (BLOCK, BLOCK), 1) <= lax.broadcasted_iota(
        jnp.int32, (BLOCK, BLOCK), 0
    )
    for step in range(rows // BLOCK):
        start = step * BLOCK
        stop = start + BLOCK
        out = None
        for head in range(2):
            mine = (lane < HD) if head == 0 else (lane >= HD)
            q_head = jnp.where(mine, query[start:stop], jnp.zeros((), bf16))
            last = jnp.where(on_diagonal, mm(q_head, key[start:stop], (1, 1)), -1e30)
            parts = [last]
            if start:
                parts = [mm(q_head, key[:start], (1, 1)), last]
            best = functools.reduce(
                jnp.maximum, [jnp.max(part, axis=1, keepdims=True) for part in parts]
            )
            parts = [jnp.exp(part - best) for part in parts]
            total = sum(jnp.sum(part, axis=1, keepdims=True) for part in parts)
            log_out[0, head, start:stop] = (best + jnp.log(total))[:, 0]
            mixed = mm(parts[-1].astype(bf16), value[start:stop], (1, 0))
            if start:
                mixed = mixed + mm(parts[0].astype(bf16), value[:start], (1, 0))
            mixed = mixed / total
            out = mixed if head == 0 else jnp.where(mine, mixed, out)
        o_out[start:stop, :] = out.astype(bf16)


def attend_back_kernel(
    q_in, k_in, v_in, g_in, log_in, cos_ref, lead_ref, trail_ref, d_out, dq_sum, dk_sum, dv_sum
):
    rows = q_in.shape[0]
    scale = HD ** (-0.5)
    lane = lax.broadcasted_iota(jnp.int32, (BLOCK, LANES), 1)
    on_diagonal = lax.broadcasted_iota(jnp.int32, (BLOCK, BLOCK), 0) <= lax.broadcasted_iota(
        jnp.int32, (BLOCK, BLOCK), 1
    )
    dk_sum[...] = jnp.zeros_like(dk_sum)
    dv_sum[...] = jnp.zeros_like(dv_sum)
    key_all = k_in[...]
    value_all = v_in[...]
    zero = jnp.zeros((), bf16)
    for step in range(rows // BLOCK):
        start = step * BLOCK
        stop = start + BLOCK
        d_query = None
        for head in range(2):
            mine = (lane < HD) if head == 0 else (lane >= HD)
            q_head = jnp.where(mine, q_in[start:stop], zero)
            g_head = jnp.where(mine, g_in[start:stop], zero)
            log_row = log_in[0, head : head + 1, start:stop]
            last = jnp.where(
                on_diagonal, jnp.exp(mm(key_all[start:stop], q_head, (1, 1)) - log_row), 0.0
            )
            probs = [(start, stop, last)]
            if start:
                probs.append((0, start, jnp.exp(mm(key_all[:start], q_head, (1, 1)) - log_row)))
            grads = [mm(value_all[lo:hi], g_head, (1, 1)) for lo, hi, _ in probs]
            delta = sum(
                jnp.sum(prob * grad, axis=0, keepdims=True)
                for (_, _, prob), grad in zip(probs, grads)
            )
            part = None
            for (lo, hi, prob), grad in zip(probs, grads):
                d_score = (prob * (grad - delta)).astype(bf16)
                dv_sum[lo:hi, :] += mm(prob.astype(bf16), g_head, (1, 0))
                dk_sum[lo:hi, :] += mm(d_score, q_head, (1, 0))
                added = mm(d_score, key_all[lo:hi], (0, 0))
                part = added if part is None else part + added
            d_query = part if head == 0 else jnp.where(mine, part, d_query)
        dq_sum[start:stop, :] = d_query * scale
    cos_t, lead, trail = cos_ref[...].T, lead_ref[...].T, trail_ref[...].T
    width = d_out.shape[1] // 3

    def put(which, vals):
        first = pl.multiple_of(which * width + pl.program_id(1) * LANES, LANES)
        d_out[:, pl.ds(first, LANES)] = vals.astype(bf16)

    put(0, unrotated(dq_sum[...], cos_t, lead, trail))
    put(1, unrotated(dk_sum[...], cos_t, lead, trail))
    put(2, dv_sum[...])


def attend(mixed_qkv, bias, tables, seqs):
    rows, width = mixed_qkv.shape[0] // seqs, mixed_qkv.shape[1] // 3
    pairs = width // LANES

    def part(which):
        return pl.BlockSpec((rows, LANES), lambda s, p: (s, which * pairs + p))

    block = pl.BlockSpec((rows, LANES), lambda s, p: (s, p))
    table = pl.BlockSpec((LANES, rows), lambda s, p: (0, s))
    low = jax.ShapeDtypeStruct((seqs * rows, width), bf16)
    return pl.pallas_call(
        attend_kernel,
        grid=(seqs, pairs),
        in_specs=[part(0), part(1), part(2), pl.BlockSpec((3, LANES), lambda s, p: (0, p))]
        + [table] * 3,
        out_specs=[block] * 4 + [pl.BlockSpec((1, 2, rows), lambda s, p: (s * pairs + p, 0, 0))],
        out_shape=[low] * 4 + [jax.ShapeDtypeStruct((seqs * pairs, 2, rows), f32)],
        compiler_params=pltpu.CompilerParams(vmem_limit_bytes=GRANT),
        cost_estimate=pl.CostEstimate(flops=20 * 10**9, bytes_accessed=10**7, transcendentals=0),
        name="attend",
    )(mixed_qkv, mixed_qkv, mixed_qkv, bias, *tables)


def attend_back(query, key, value, back, log_total, tables, seqs):
    rows, width = query.shape[0] // seqs, query.shape[1]
    pairs = width // LANES
    block = pl.BlockSpec((rows, LANES), lambda s, p: (s, p))
    table = pl.BlockSpec((LANES, rows), lambda s, p: (0, s))
    return pl.pallas_call(
        attend_back_kernel,
        grid=(seqs, pairs),
        in_specs=[block] * 4
        + [pl.BlockSpec((1, 2, rows), lambda s, p: (s * pairs + p, 0, 0))]
        + [table] * 3,
        out_specs=pl.BlockSpec((rows, 3 * width), lambda s, p: (s, 0)),
        out_shape=jax.ShapeDtypeStruct((seqs * rows, 3 * width), bf16),
        scratch_shapes=[pltpu.VMEM((rows, LANES), f32)] * 3,
        compiler_params=pltpu.CompilerParams(vmem_limit_bytes=GRANT),
        cost_estimate=pl.CostEstimate(flops=30 * 10**9, bytes_accessed=10**7, transcendentals=0),
        name="attend_back",
    )(query, key, value, back, log_total, *tables)


def bits_of(count):
    bits = []
    bit = 1
    while bit < count:
        bits.append(bit)
        bit *= 2
    return bits


def flipped(index, bit):
    return index + bit * (1 - 2 * ((index // bit) % 2))


def run_chains(chains):
    chains = [chain for chain in chains]
    for chain in chains:
        next(chain)
    while chains:
        left = []
        for chain in chains:
            try:
                next(chain)
                left.append(chain)
            except StopIteration:
                pass
        chains = left


class Sems:
    def __init__(self, send, recv):
        self.send, self.recv, self.used = send, recv, 0

    def take(self):
        self.used += 1
        return self.send.at[self.used - 1], self.recv.at[self.used - 1]


def remote(src, dst, sems, target):
    return pltpu.make_async_remote_copy(
        src_ref=src,
        dst_ref=dst,
        send_sem=sems[0],
        recv_sem=sems[1],
        device_id=target,
        device_id_type=pl.DeviceIdType.MESH,
    )


def greet(ctx, dp):
    here, mine = lax.axis_index("ctx"), lax.axis_index("dp")
    barrier = pltpu.get_barrier_semaphore()
    targets = [{"ctx": lax.rem(here + by, ctx)} for by in range(1, ctx)]
    targets += [{"dp": flipped(mine, bit)} for bit in bits_of(dp)]
    for target in targets:
        pl.semaphore_signal(barrier, inc=1, device_id=target, device_id_type=pl.DeviceIdType.MESH)
    pl.semaphore_wait(barrier, len(targets))


def line_chain(src, out, sems, ctx):
    here = lax.axis_index("ctx")
    ups = [sems.take() for _ in range(1, ctx)]
    downs = [sems.take() for _ in range(1, ctx)]

    def hop(block, slot, step, going):
        by = 1 if going is ups else -1
        return remote(block, out.at[slot], going[step], {"ctx": here + by})

    @pl.when(here < ctx - 1)
    def _():
        hop(src, here, 0, ups).start()

    @pl.when(here > 0)
    def _():
        hop(src, here, 0, downs).start()

    yield
    for step in range(1, ctx):
        for going, sign in ((ups, -1), (downs, 1)):
            slot = here + sign * step
            inside = (slot >= 0) if sign < 0 else (slot < ctx)
            more = (here < ctx - 1) if sign < 0 else (here > 0)
            if step < ctx - 1:

                @pl.when(jnp.logical_and(inside, more))
                def _():
                    hop(out.at[slot], slot, step - 1, going).wait_recv()
                    hop(out.at[slot], slot, step, going).start()

                @pl.when(jnp.logical_and(inside, jnp.logical_not(more)))
                def _():
                    hop(out.at[slot], slot, step - 1, going).wait_recv()

            else:

                @pl.when(inside)
                def _():
                    hop(out.at[slot], slot, step - 1, going).wait_recv()

        yield

    for step in range(ctx - 1):
        for going, sign in ((ups, -1), (downs, 1)):
            slot = here + sign * step
            inside = (slot >= 0) if sign < 0 else (slot < ctx)
            more = (here < ctx - 1) if sign < 0 else (here > 0)

            @pl.when(jnp.logical_and(inside, more))
            def _():
                hop(out.at[slot], slot, step, going).wait_send()


def weight_chain(cuts, out, sems, own_sem, ctx, dp):
    here, mine = lax.axis_index("ctx"), lax.axis_index("dp")
    rows = cuts[0][0].shape[0]
    slab = rows * ctx
    half = slab // 2

    def piece(owner, cut):
        at = pl.ds(pl.multiple_of((mine * ctx + owner) * rows, rows), rows)
        return out.at[at, pl.ds(cut[3], cut[1])]

    def taken(peer, cut):
        block, width, first, _ = cut
        if first is None:
            return block
        return block.at[:, pl.ds(pl.multiple_of(first + peer * width, LANES), width)]

    def part(owner, which):
        return out.at[pl.ds(pl.multiple_of(owner * slab + which * half, half), half)]

    trades, own = [], []
    for by in range(1, ctx):
        peer = lax.rem(here + by, ctx)
        source = lax.rem(here + ctx - by, ctx)
        for cut in cuts:
            sem = sems.take()
            copy = remote(taken(peer, cut), piece(here, cut), sem, {"ctx": peer})
            copy.start()
            trades.append((copy, remote(taken(peer, cut), piece(source, cut), sem, {"ctx": peer})))
    for index, cut in enumerate(cuts):
        copy = pltpu.make_async_copy(taken(here, cut), piece(here, cut), own_sem.at[index])
        copy.start()
        own.append(copy)
    yield
    for _, arrival in trades:
        arrival.wait_recv()
    for copy in own:
        copy.wait()
    far = bits_of(dp)[1:]
    orders = [far + [1], far[::-1] + [1]]
    held = [[mine], [mine]]
    sent = []
    for stage in range(len(far) + 1):
        arrivals = []
        for which in range(2):
            bit = orders[which][stage]
            for owner in list(held[which]):
                sem = sems.take()
                copy = remote(part(owner, which), part(owner, which), sem, {"dp": flipped(mine, bit)})
                copy.start()
                sent.append(copy)
                coming = flipped(owner, bit)
                arrivals.append(remote(part(coming, which), part(coming, which), sem, {"dp": flipped(mine, bit)}))
                held[which].append(coming)
        yield
        for arrival in arrivals:
            arrival.wait_recv()
    for copy, _ in trades:
        copy.wait_send()
    for copy in sent:
        copy.wait_send()


def cuts_of(blocks, ctx):
    qkv, fc1, out, fc2, small = blocks
    head_cols, ff_cols = D // ctx, FF // ctx
    first = [(qkv, head_cols, part * D, part * head_cols) for part in range(3)]
    first.append((fc1, ff_cols, 0, 3 * head_cols))
    return [first, [(out, head_cols, 0, 0), (fc2, ff_cols, 0, head_cols)], [(small, LANES, None, 0)]]


def gather_kernel(ctx, dp, seqs, *refs):
    tokens, places, blocks = refs[0], refs[1], refs[2:7]
    tok_out, place_out, outs = refs[7], refs[8], refs[9:12]
    send, recv, own_sems, tok_sems = refs[12:]
    here = lax.axis_index("ctx")
    sems = Sems(send, recv)
    greet(ctx, dp)
    chains = [line_chain(places, place_out, sems, ctx)]
    for group, cuts in enumerate(cuts_of(blocks, ctx)):
        chains.append(weight_chain(cuts, outs[group], sems, own_sems.at[group], ctx, dp))
        if group < seqs:
            chains.append(line_chain(tokens.at[group], tok_out.at[group], sems, ctx))
    local = [
        pltpu.make_async_copy(tokens.at[seq], tok_out.at[seq, here], tok_sems.at[seq])
        for seq in range(seqs)
    ]
    local.append(pltpu.make_async_copy(places, place_out.at[here], tok_sems.at[seqs]))
    for copy in local:
        copy.start()
    run_chains(chains)
    for copy in local:
        copy.wait()


def gather_all(tokens, places, blocks, ctx, dp):
    seqs, span = tokens.shape[0], tokens.shape[1]
    rows = blocks[0].shape[0] * ctx * dp
    head_cols, ff_cols = D // ctx, FF // ctx
    copies = (seqs + 1) * 2 * (ctx - 1) + 7 * (ctx - 1) + 3 * 2 * (dp - 1)
    hbm = pl.BlockSpec(memory_space=pl.ANY)
    outs = pl.pallas_call(
        functools.partial(gather_kernel, ctx, dp, seqs),
        in_specs=[hbm] * 7,
        out_specs=[hbm] * 5,
        out_shape=[
            jax.ShapeDtypeStruct((seqs, ctx, span, D), bf16),
            jax.ShapeDtypeStruct((ctx,) + places.shape, f32),
            jax.ShapeDtypeStruct((rows, 3 * head_cols + ff_cols), bf16),
            jax.ShapeDtypeStruct((rows, head_cols + ff_cols), bf16),
            jax.ShapeDtypeStruct((rows, LANES), bf16),
        ],
        scratch_shapes=[
            pltpu.SemaphoreType.DMA((copies,)),
            pltpu.SemaphoreType.DMA((copies,)),
            pltpu.SemaphoreType.DMA((3, 4)),
            pltpu.SemaphoreType.DMA((seqs + 1,)),
        ],
        compiler_params=pltpu.CompilerParams(collective_id=1, has_side_effects=True),
        name="gather_all",
    )(tokens, places, *blocks)
    return outs[0], outs[1], outs[2:]


def add_into(target, other, rows):
    step = 32

    @pl.loop(0, rows // step)
    def _(index):
        here = pl.ds(pl.multiple_of(index * step, step), step)
        target[here, :] = target[here, :] + other[here, :]


def without(pattern, bit):
    return tuple(item for item in pattern if item != bit)


def patterns_of(bits):
    found = [()]
    for bit in bits:
        found += [pattern + (bit,) for pattern in found]
    return found


def owner_of(mine, pattern):
    for bit in pattern:
        mine = flipped(mine, bit)
    return mine


def patterns_for(dp):
    return sorted(patterns_of(bits_of(dp)[1:]), key=len, reverse=True)


class Slabs:
    def __init__(self, plan, x_v, turned, x_sems):
        self.plan, self.x_v, self.turned, self.x_sems = plan, x_v, turned, x_sems
        self.next = 0
        for index in (0, 1):
            self.start(index)
        self.wait(0)
        turned[0] = x_v[0].T

    def copies(self, index):
        arrays, owner = self.plan[index]
        slab = self.turned.shape[1]
        at = pl.ds(pl.multiple_of(owner * slab, LANES), slab)
        found = []
        for seq, array in enumerate(arrays):
            length = array.shape[0]
            found.append(
                pltpu.make_async_copy(
                    array.at[:, at],
                    self.x_v.at[index % 2, pl.ds(seq * length, length)],
                    self.x_sems.at[index % 2, seq],
                )
            )
        return found

    def start(self, index):
        for copy in self.copies(index):
            copy.start()

    def wait(self, index):
        for copy in self.copies(index):
            copy.wait()

    def multiply(self, y_v, cols, store):
        index = self.next
        self.next += 1
        more = index + 1 < len(self.plan)
        if index + 2 < len(self.plan):
            self.start(index + 2)
        if more:
            self.wait(index + 1)
        tile, rows = cols // 2, self.turned.shape[2] // 2

        @pl.loop(0, 2)
        def _(part):
            at = pl.ds(pl.multiple_of(part * tile, LANES), tile)
            if more:
                some = pl.ds(pl.multiple_of(part * rows, rows), rows)
                self.turned[(index + 1) % 2, :, some] = self.x_v[(index + 1) % 2, some, :].T
            store(at, mm(self.turned[index % 2], y_v[:, at], (1, 0)))


def pooled_chain(ys, parts, slabs, boxes, land_core, lands, sems, y_v, y_sems, own_sem, ctx, dp):
    here, mine = lax.axis_index("ctx"), lax.axis_index("dp")
    slab, cols = land_core.shape[1:]
    rows, half = slab // ctx, slab // 2
    far = bits_of(dp)[1:]
    patterns = patterns_for(dp)
    partner = flipped(mine, 1)
    loads = []
    for arrays, first in ys:
        for seq, array in enumerate(arrays):
            length, width = array.shape
            loads.append(
                pltpu.make_async_copy(
                    array,
                    y_v.at[pl.ds(seq * length, length), pl.ds(first, width)],
                    y_sems.at[len(loads)],
                )
            )
    for load in loads:
        load.start()
    for load in loads:
        load.wait()
    sent = []
    for index in range(len(patterns)):
        if boxes["sent"][index] is not None:
            boxes["sent"][index].wait_send()
        box = boxes["box"].at[index, :, pl.ds(0, cols)]

        def store(at, vals, index=index):
            boxes["box"][index, :, at] = vals.astype(bf16)

        slabs.multiply(y_v, cols, store)
        copy = remote(box, land_core.at[index], sems.take(), {"dp": partner})
        copy.start()
        boxes["sent"][index] = copy
        sent.append(copy)
    yield
    arrived, sent = sent, []
    held, coming = [{}, {}], [[], []]
    orders = [far, far[::-1]]
    used = 0

    def pass_on(which, stage, pattern, block):
        nonlocal used
        bit = orders[which][stage]
        copy = remote(block, lands.at[used], sems.take(), {"dp": flipped(mine, bit)})
        copy.start()
        sent.append(copy)
        coming[which].append((copy, lands.at[used], without(pattern, bit)))
        used += 1

    for index, pattern in enumerate(patterns):
        arrived[index].wait_recv()

        def store(at, vals, index=index):
            land_core[index, :, at] = (vals + land_core[index, :, at].astype(f32)).astype(bf16)

        slabs.multiply(y_v, cols, store)
        for which in range(2):
            block = land_core.at[index, pl.ds(which * half, half)]
            if orders[which][0] in pattern:
                pass_on(which, 0, pattern, block)
            else:
                held[which][pattern] = block
        if index == len(patterns) // 2 - 1:
            yield
    for stage in range(len(far)):
        yield
        for which in range(2):
            kept, arrivals = {}, coming[which]
            coming[which] = []
            for copy, landing, pattern in arrivals:
                copy.wait_recv()
                add_into(landing, held[which][pattern], half)
                if stage + 1 < len(far) and orders[which][stage + 1] in pattern:
                    pass_on(which, stage + 1, pattern, landing)
                else:
                    kept[pattern] = landing
            held[which] = kept
    final = [held[0][()], held[1][()]]
    trades = []

    def piece(which, peer, part):
        first = pl.multiple_of(peer * rows - which * half, rows)
        return final[which].at[pl.ds(first, rows), pl.ds(part[1], part[2])]

    def target(source, part):
        first = pl.multiple_of(part[3] + source * part[2], LANES)
        return part[0].at[:, pl.ds(first, part[2])]

    for by in range(1, ctx):
        peer = lax.rem(here + by, ctx)
        source = lax.rem(here + ctx - by, ctx)
        for part in parts:
            sem = sems.take()
            for which in range(2):

                @pl.when(peer // (ctx // 2) == which)
                def _():
                    remote(piece(which, peer, part), target(here, part), sem, {"ctx": peer}).start()

            trades.append((sem, peer, source, part))
    for which in range(2):

        @pl.when(here // (ctx // 2) == which)
        def _():
            for part in parts:
                copy = pltpu.make_async_copy(piece(which, here, part), target(here, part), own_sem)
                copy.start()
                copy.wait()

    yield
    for sem, peer, source, part in trades:
        some = final[0].at[pl.ds(0, rows), pl.ds(part[1], part[2])]
        remote(some, target(source, part), sem, {"ctx": peer}).wait_recv()
    for sem, peer, source, part in trades:
        some = final[0].at[pl.ds(0, rows), pl.ds(part[1], part[2])]
        remote(some, target(source, part), sem, {"ctx": peer}).wait_send()
    for copy in sent:
        copy.wait_send()


def sum_chain(partial, out, held, downs_land, ups_land, sems, load_sem, ctx):
    here = lax.axis_index("ctx")
    rows = held.shape[0] // ctx
    load = pltpu.make_async_copy(partial, held, load_sem)
    load.start()
    down_sems = [sems.take() for _ in range(1, ctx)]
    up_sems = [sems.take() for _ in range(1, ctx)]

    def chunk(index):
        return held.at[pl.ds(pl.multiple_of(index * rows, rows), rows)]

    def hop(block, step, down):
        lands, going = (downs_land, down_sems) if down else (ups_land, up_sems)
        by = -1 if down else 1
        return remote(block, lands.at[step - 1], going[step - 1], {"ctx": here + by})

    load.wait()

    @pl.when(here == ctx - 1)
    def _():
        for step in range(1, ctx):
            hop(chunk(step - 1), step, True).start()

    @pl.when(here == 0)
    def _():
        for step in range(1, ctx):
            hop(chunk(ctx - step), step, False).start()

    yield
    for step in range(2, ctx):

        @pl.when(jnp.logical_and(here < ctx - 1, here + step - ctx >= 0))
        def _():
            block = downs_land.at[step - 2]
            hop(block, step - 1, True).wait_recv()
            add_into(block, chunk(here + step - ctx), rows)
            hop(block, step, True).start()

        @pl.when(jnp.logical_and(here > 0, here + ctx - step <= ctx - 1))
        def _():
            block = ups_land.at[step - 2]
            hop(block, step - 1, False).wait_recv()
            add_into(block, chunk(here + ctx - step), rows)
            hop(block, step, False).start()

        yield

    @pl.when(here < ctx - 1)
    def _():
        hop(downs_land.at[ctx - 2], ctx - 1, True).wait_recv()

    @pl.when(here > 0)
    def _():
        hop(ups_land.at[ctx - 2], ctx - 1, False).wait_recv()

    step = 32

    @pl.loop(0, rows // step)
    def _(index):
        at = pl.ds(pl.multiple_of(index * step, step), step)
        mine = held[pl.ds(pl.multiple_of(here * rows + index * step, step), step), :].astype(f32)
        down = downs_land[ctx - 2, at, :].astype(f32)
        up = ups_land[ctx - 2, at, :].astype(f32)
        out[at, :] = (
            mine + jnp.where(here < ctx - 1, down, 0.0) + jnp.where(here > 0, up, 0.0)
        )

    for step in range(1, ctx):

        @pl.when(here + step - ctx >= 0)
        def _():
            hop(chunk(0), step, True).wait_send()

        @pl.when(here + ctx - step <= ctx - 1)
        def _():
            hop(chunk(0), step, False).wait_send()


def reduce_kernel(ctx, dp, seqs, *refs):
    partial, normal, attended, hidden, cot, d_qkv, d_pre = ([ref] for ref in refs[:7])
    length = partial[0].shape[0] // seqs
    partial = partial[0].at[pl.ds((seqs - 1) * length, length)]
    refs = refs[7:]
    sum_out, qkv_out, fc1_out, out_out, fc2_out = refs[:5]
    held, downs_land, ups_land, box, x_v, turned, y_v = refs[5:12]
    land_core, lands = refs[12:15], refs[15:18]
    send, recv, load_sem, x_sems, y_sems, own_sems = refs[18:]
    head_cols, ff_cols = D // ctx, FF // ctx
    parts = [
        [(out_out, 0, head_cols, 0), (fc2_out, head_cols, ff_cols, 0)],
        [(fc1_out, 0, ff_cols, 0)],
        [(qkv_out, part * head_cols, head_cols, part * D) for part in range(3)],
    ]
    ys = [[(attended, 0), (hidden, head_cols)], [(d_pre, 0)], [(d_qkv, 0)]]
    mine = lax.axis_index("dp")
    plan = []
    for arrays in (cot, normal, normal):
        for first in (flipped(mine, 1), mine):
            plan += [(arrays, owner_of(first, pattern)) for pattern in patterns_for(dp)]
    sems = Sems(send, recv)
    greet(ctx, dp)
    slabs = Slabs(plan, x_v, turned, x_sems)
    boxes = {"box": box, "sent": [None] * (dp // 2)}
    line = sum_chain(partial, sum_out, held, downs_land, ups_land, sems, load_sem, ctx)
    groups = [
        pooled_chain(
            ys[group], parts[group], slabs, boxes, land_core[group], lands[group],
            sems, y_v, y_sems, own_sems.at[group], ctx, dp,
        )
        for group in range(3)
    ]
    first, second, third = groups
    order = [line, first, first, first, second, first, line, second, second, first]
    order += [third, second, line, third, third, first, second, third, third, second, line, third, line]
    run_in(order, [line] + groups)
    for copy in boxes["sent"]:
        copy.wait_send()


def run_in(order, chains):
    ended = set()
    turn = 0
    while len(ended) < len(chains):
        chain = order[turn] if turn < len(order) else chains[(turn - len(order)) % len(chains)]
        turn += 1
        if id(chain) in ended:
            continue
        try:
            next(chain)
        except StopIteration:
            ended.add(id(chain))


def reduce_all(partial, normal, attended, hidden, cot, d_qkv, d_pre, seqs, ctx, dp):
    length = partial.shape[0] // seqs
    rows = length // ctx
    slab = D // dp
    copies = 2 * (ctx - 1) + 3 * (dp // 2 + dp - 2) + 6 * (ctx - 1)
    hbm = pl.BlockSpec(memory_space=pl.ANY)
    vmem = pl.BlockSpec(memory_space=pltpu.VMEM)
    head_cols, ff_cols = D // ctx, FF // ctx
    cols = [head_cols + ff_cols, ff_cols, 3 * head_cols]
    outs = pl.pallas_call(
        functools.partial(reduce_kernel, ctx, dp, seqs),
        in_specs=[hbm] * 7,
        out_specs=[vmem] + [hbm] * 4,
        out_shape=[jax.ShapeDtypeStruct((rows, partial.shape[1]), f32)]
        + [jax.ShapeDtypeStruct((slab // ctx, width), bf16) for width in (3 * D, FF, D, FF)],
        scratch_shapes=[pltpu.VMEM((length, partial.shape[1]), bf16)]
        + [pltpu.VMEM((ctx - 1, rows, partial.shape[1]), bf16)] * 2
        + [
            pltpu.VMEM((dp // 2, slab, cols[0]), bf16),
            pltpu.VMEM((2, seqs * length, slab), bf16),
            pltpu.VMEM((2, slab, seqs * length), bf16),
            pltpu.VMEM((seqs * length, cols[0]), bf16),
        ]
        + [pltpu.VMEM((dp // 2, slab, width), bf16) for width in cols]
        + [pltpu.VMEM((dp - 2, slab // 2, width), bf16) for width in cols]
        + [
            pltpu.SemaphoreType.DMA((copies,)),
            pltpu.SemaphoreType.DMA((copies,)),
            pltpu.SemaphoreType.DMA,
            pltpu.SemaphoreType.DMA((2, seqs)),
            pltpu.SemaphoreType.DMA((2 * seqs,)),
            pltpu.SemaphoreType.DMA((3,)),
        ],
        compiler_params=pltpu.CompilerParams(
            collective_id=2, has_side_effects=True, vmem_limit_bytes=GRANT
        ),
        cost_estimate=pl.CostEstimate(flops=150 * 10**9, bytes_accessed=10**8, transcendentals=0),
        name="reduce_all",
    )(partial, normal, attended, hidden, cot, d_qkv, d_pre)
    return outs[0], outs[1:]


def normalised(rows_in):
    row_mean = jnp.mean(rows_in, axis=-1, keepdims=True)
    centred = rows_in - row_mean
    variance = jnp.mean(centred * centred, axis=-1, keepdims=True)
    inv_std = lax.rsqrt(variance + 1e-05)
    return centred * inv_std, inv_std


def gelu_both(pre):
    return jax.vjp(lambda vals: jax.nn.gelu(vals, approximate=True), pre)


def per_device(
    tokens,
    cotangent,
    positions,
    wqkv_master,
    fc1_master,
    out_master,
    fc2_master,
    small_master,
    wqkv_first,
    wqkv_second,
    fc1_first,
    fc1_second,
    out_first,
    out_second,
    fc2_first,
    fc2_second,
    small_first,
    small_second,
):
    seqs, span = tokens.shape[0], tokens.shape[1]
    ctx, dp = lax.axis_size("ctx"), lax.axis_size("dp")
    ctx_index = lax.axis_index("ctx")
    length = span * ctx
    total_rows = seqs * length
    own_rows = wqkv_master.shape[0]
    head_cols, ff_cols = D // ctx, FF // ctx

    gate = lax.optimization_barrier
    small_low = jnp.pad(small_master.astype(bf16), ((0, 0), (0, LANES - small_master.shape[1])))
    blocks = [wqkv_master, fc1_master, out_master, fc2_master]
    blocks = [block.astype(bf16) for block in blocks] + [small_low]
    places = jnp.pad(positions.astype(f32).reshape(-1, LANES), ((0, 8 - seqs * span // LANES), (0, 0)))
    tok_all, place, (in_w, of_w, small_all) = gather_all(tokens, places, blocks, ctx, dp)
    qkv_w, fc1_w = in_w[:, : 3 * head_cols], in_w[:, 3 * head_cols :]
    params = small_all[:, :16].astype(f32)
    place = place[:, : seqs * span // LANES].reshape(ctx, seqs, span)
    place = jnp.transpose(place, (1, 0, 2)).reshape(total_rows)
    half_rot = ROT // 2
    exponent = jnp.arange(half_rot, dtype=f32) * (-2.0 / ROT)
    frequency = jnp.power(f32(10000.0), exponent)
    angles = frequency[:, None] * place[None, :]
    cos_s, sin_s = jnp.cos(angles), jnp.sin(angles)
    none = jnp.zeros_like(cos_s)
    rest = jnp.zeros((HD - ROT, total_rows), f32)
    tables = [
        jnp.concatenate([cos_s, cos_s, rest + 1.0] * 2, axis=0),
        jnp.concatenate([-sin_s, none, rest] * 2, axis=0),
        jnp.concatenate([none, sin_s, rest] * 2, axis=0),
    ]

    def my_part(values, cols):
        return lax.dynamic_slice_in_dim(values, ctx_index * cols, cols, values.ndim - 1)

    qkv_bias = my_part(params[:, 2:5].T, head_cols)
    fc1_bias = my_part(params[:, 6:10].T.reshape(FF), ff_cols)
    gain, shift = params[:, 0], params[:, 1]
    def scattered(partial):
        return lax.psum_scatter(partial, "ctx", scatter_dimension=1, tiled=True).astype(f32)

    cot, tok_all = gate((cotangent, tok_all))
    cot_all = lax.all_gather(cot, "ctx", axis=1, tiled=True).reshape(total_rows, D)
    normal_low = normalised(tok_all.reshape(total_rows, D).astype(f32))[0]
    normal_low = (normal_low * gain + shift).astype(bf16)
    projected = mm(normal_low, in_w[:, : 3 * head_cols], (1, 0))
    query, key, value, attended, log_total = attend(projected, qkv_bias, tables, seqs)
    pre = mm(normal_low, in_w[:, 3 * head_cols :], (1, 0)) + fc1_bias
    hidden = gelu_both(pre)[0].astype(bf16)
    branch = mm(jnp.concatenate([attended, hidden], axis=1), of_w, (1, 1)).astype(bf16)
    pre, hidden, branch, cot_all = gate((pre, hidden, branch, cot_all))
    mix = scattered(branch.reshape(seqs, length, D))
    back = mm(cot_all, of_w[:, :head_cols], (1, 0)).astype(bf16)
    grad_hidden = mm(cot_all, of_w[:, head_cols:], (1, 0))
    d_pre = gelu_both(pre)[1](grad_hidden)[0].astype(bf16)
    d_qkv = attend_back(query, key, value, back, log_total, tables, seqs)
    d_part = mm(jnp.concatenate([d_qkv, d_pre], axis=1), in_w, (1, 1)).astype(bf16)
    sum_qkv, sum_pre = (jnp.sum(part, axis=0, dtype=f32) for part in (d_qkv, d_pre))
    d_qkv, d_pre, d_part, mix, sum_qkv, sum_pre = gate(
        (d_qkv, d_pre, d_part, mix, sum_qkv, sum_pre)
    )
    others = scattered(d_part[: total_rows - length].reshape(seqs - 1, length, D))
    sum_out = jnp.sum(cotangent.astype(f32), axis=(0, 1))[None]
    normed, inv_std = normalised(tokens.astype(f32))
    last, grads = reduce_all(
        d_part, normal_low, attended, hidden, cot_all, d_qkv, d_pre, seqs, ctx, dp
    )
    d_normal = [others[seq] for seq in range(seqs - 1)] + [last]

    def spread(sums, count, cols):
        whole = jnp.zeros((count, ctx * cols), f32)
        return lax.dynamic_update_slice_in_dim(whole, sums.reshape(count, cols), ctx_index * cols, 1)

    sum_qkv = spread(sum_qkv, 3, head_cols)
    sum_pre = spread(sum_pre, 1, ff_cols).reshape(4, D)
    gain_terms = sum(jnp.sum(part * normed[seq], axis=0) for seq, part in enumerate(d_normal))[None]
    shift_terms = sum(jnp.sum(part, axis=0) for part in d_normal)[None]
    small_terms = jnp.concatenate(
        [gain_terms, shift_terms, sum_qkv, sum_out, sum_pre, sum_out], axis=0
    )
    small_sent = jnp.transpose(small_terms.reshape(11, ctx * dp, own_rows), (1, 0, 2))
    small_sent, d_normal, grads, mix = gate((small_sent, d_normal, grads, mix))
    small_got = lax.all_to_all(small_sent.reshape(ctx * dp, 1, 11 * own_rows), EVERY, 0, 0, tiled=True)
    small_grad = jnp.sum(small_got, axis=(0, 1)).reshape(11, own_rows).T

    qkv_grad, fc1_grad, out_grad, fc2_grad = (grad.astype(f32) for grad in grads)
    mixed = (tokens.astype(f32) + mix + params[:, 5] + params[:, 10]).astype(bf16)
    d_scaled = jnp.stack(d_normal) * gain
    input_grad = cotangent.astype(f32) + inv_std * (
        d_scaled
        - jnp.mean(d_scaled, axis=-1, keepdims=True)
        - normed * jnp.mean(d_scaled * normed, axis=-1, keepdims=True)
    )
    qkv_new = adamw(wqkv_master, wqkv_first, wqkv_second, qkv_grad, 0.04, 0.1)
    fc1_new = adamw(fc1_master, fc1_first, fc1_second, fc1_grad, 0.04, 0.1)
    out_new = adamw(out_master, out_first, out_second, out_grad, 0.4, 0.1)
    fc2_new = adamw(fc2_master, fc2_first, fc2_second, fc2_grad, 0.02, 0.1)
    small_new = adamw(small_master, small_first, small_second, small_grad, 0.3, 0.0)
    return (mixed, input_grad, *qkv_new, *fc1_new, *out_new, *fc2_new, *small_new)


def solution(mesh):
    split = P("dp", "ctx", None)
    rows = P(("dp", "ctx"), None)
    return jax.shard_map(
        per_device,
        mesh=mesh,
        in_specs=(split, split, P("dp", "ctx")) + (rows,) * 15,
        out_specs=(split, split) + (rows,) * 15,
        check_vma=False,
    )
```

profile of v0, /device:TPU:0, one launch (start us, length us, event | category | flops | bytes accessed | tf_op | source)
XLA Modules:
  0.0 773.1 jit_solution(15968664817663188731)
XLA Ops:
  16.3 200.9 %gather_all.1 = (bf16[2,4,256,2048]{3,2,1,0:T(8,128)(2,1)}, f32[4,8,128]{2,1,0:T(8,128)}, bf16[2048,3584]{1,0:T(8,128)(2,1)}, bf16[2048,2560]{1,0:T(8,128)(2,1)}, bf16[2048,128]{1,0:T(8,128)(2,1)}) custom-call(bf16[2,256,2048]{2,1,0:T(8,128)(2,1)} %refs_0_.1, f32[8,128]{1,0:T(8,128)} %pad.8.refs_1_, bf16[64,6144]{1,0:T(8,128)(2,1)} %convert_element_type.90.refs_2_, ...), custom_call_target="tpu_custom_call" | custom-call | tf_op jit(solution)/shard_map/gather_all/pallas_call | solution.py:407
  219.3 4.7 convert_reduce_fusion.2
  232.2 6.5 fusion.18.refs_1_
  238.7 3.2 copy-done.10
  241.9 17.6 %fusion.38.q_in.k_in.v_in = f32[2048,1536]{1,0:T(8,128)} fusion(bf16[2048,2048]{1,0:T(8,128)(2,1)S(1)} %fusion.18.refs_1_, bf16[2048,3584]{1,0:T(8,128)(2,1)} %get-tuple-element.55), kind=kOutput, calls=%fused_computation.41 | convolution fusion | flops 12884901888 | bytes 27262976 | tf_op jit(solution)/shard_map/dot_general | solution.py:41
  259.5 35.0 %attend.1 = (bf16[2048,512]{1,0:T(8,128)(2,1)}, bf16[2048,512]{1,0:T(8,128)(2,1)}, bf16[2048,512]{1,0:T(8,128)(2,1)}, bf16[2048,512]{1,0:T(8,128)(2,1)}, f32[8,2,1024]{2,1,0:T(2,128)}) custom-call(f32[2048,1536]{1,0:T(8,128)} %fusion.38.q_in.k_in.v_in, f32[2048,1536]{1,0:T(8,128)} %fusion.38.q_in.k_in.v_in, f32[2048,1536]{1,0:T(8,128)} %fusion.38.q_in.k_in.v_in, ...), custom_call_target="tpu_custom_call" | custom-call | flops 20000000000 | bytes 10000000 | tf_op jit(solution)/shard_map/attend/pallas_call | solution.py:163
  294.5 29.6 %fusion.14 = (bf16[2048,2048]{1,0:T(8,128)(2,1)}, f32[2048,2048]{1,0:T(8,128)}) fusion(f32[2048]{0:T(1024)S(1)} %dynamic_slice.7, bf16[2048,2048]{1,0:T(8,128)(2,1)} %copy-done.10, bf16[2048,3584]{1,0:T(8,128)(2,1)} %get-tuple-element.55), kind=kOutput, calls=%fused_computation.17 | convolution fusion | flops 17221812224 | bytes 41951232 | tf_op jit(solution)/shard_map/dot_general | solution.py:41
  324.0 28.3 %fusion.32 = bf16[2048,2048]{1,0:T(8,128)(2,1)} fusion(bf16[2048,2560]{1,0:T(8,128)(2,1)} %get-tuple-element.61, bf16[2048,2048]{1,0:T(8,128)(2,1)} %get-tuple-element.68.refs_3_, bf16[2048,512]{1,0:T(8,128)(2,1)S(1)} %copy-done.46), kind=kOutput, calls=%fused_computation.39 | convolution fusion | flops 21500002304 | bytes 29360128 | tf_op jit(solution)/shard_map/dot_general | solution.py:41
  352.3 14.0 %all-gather.2.cloned.1.call-done = bf16[2,1024,2048]{2,1,0:T(8,128)(2,1)} async-done(((bf16[2,256,2048]{2,1,0:T(8,128)(2,1)}), bf16[2,1024,2048]{2,1,0:T(8,128)(2,1)}) %all-gather.2.cloned.1.call-update) | async-done | bytes 8388624 | tf_op jit(solution)/shard_map/all_gather | solution.py:882
  374.4 7.5 convolution_convert_fusion.g_in
  381.9 45.8 %attend_back.1.refs_5_ = bf16[2048,1536]{1,0:T(8,128)(2,1)} custom-call(bf16[2048,512]{1,0:T(8,128)(2,1)} %get-tuple-element.57.q_in, bf16[2048,512]{1,0:T(8,128)(2,1)} %get-tuple-element.58.k_in, bf16[2048,512]{1,0:T(8,128)(2,1)} %get-tuple-element.59.v_in, bf16[2048,512]{1,0:T(8,128)(2,1)} %convolution_convert_fusion.g_in, ...), custom_call_target="tpu_custom_call" | custom-call | flops 30000001024 | bytes 10000000 | tf_op jit(solution)/shard_map/attend_back/pallas_call | solution.py:181
  427.7 3.7 convert_reduce_fusion.1
  431.4 36.2 %convert_reduce_fusion = (f32[2048]{0:T(1024)S(1)}, bf16[2048,2048]{1,0:T(8,128)(2,1)}) fusion(f32[2048,2048]{1,0:T(8,128)} %get-tuple-element.65, bf16[2048,2048]{1,0:T(8,128)(2,1)} %bitcast.89, bf16[2048,2560]{1,0:T(8,128)(2,1)} %get-tuple-element.61), kind=kOutput, calls=%fused_computation.23 | convolution fusion | flops 17272141824 | bytes 41951232 | tf_op jit(solution)/shard_map/dot_general | solution.py:41
  467.6 38.9 %fusion.35.refs_0_ = bf16[2048,2048]{1,0:T(8,128)(2,1)} fusion(bf16[2048,3584]{1,0:T(8,128)(2,1)} %get-tuple-element.55, bf16[2048,2048]{1,0:T(8,128)(2,1)} %get-tuple-element.70.refs_6_, bf16[2048,1536]{1,0:T(8,128)(2,1)} %attend_back.1.refs_5_), kind=kOutput, calls=%fused_computation.40 | convolution fusion | flops 30098325504 | bytes 37748736 | tf_op jit(solution)/shard_map/dot_general | solution.py:41
  506.5 4.9 reduce-scatter.3.cloned.1.call-done
  511.3 4.1 convert_element_type.105
  515.5 4.8 slice_bitcast_fusion
  523.0 202.8 %reduce_all.1 = (f32[256,2048]{1,0:T(8,128)}, bf16[64,6144]{1,0:T(8,128)(2,1)}, bf16[64,8192]{1,0:T(8,128)(2,1)}, bf16[64,2048]{1,0:T(8,128)(2,1)}, bf16[64,8192]{1,0:T(8,128)(2,1)}) custom-call(bf16[2048,2048]{1,0:T(8,128)(2,1)} %fusion.35.refs_0_, bf16[2048,2048]{1,0:T(8,128)(2,1)} %copy-done.10, bf16[2048,512]{1,0:T(8,128)(2,1)} %get-tuple-element.60.refs_2_, ...), custom_call_target="tpu_custom_call" | custom-call | flops 149999992832 | bytes 100000000 | tf_op jit(solution)/shard_map/reduce_all/pallas_call | solution.py:776
  726.0 4.0 fusion.52
  734.8 7.3 all-to-all-start
  742.2 5.5 multiply_subtract_fusion.2
  747.9 3.9 multiply_subtract_fusion.1
  753.3 3.9 multiply_subtract_fusion
  759.7 4.2 convert_add_fusion.1
  (179 shorter events, 41.1 us)
Async XLA Ops:
  7.2 6.0 copy-start.14
  7.2 6.7 copy-start.12
  7.2 359.1 %all-gather.2.cloned.1.call-start = ((), (), s32[]{:S(2)}) async-start(), calls=%async_computation.3 | async-start | bytes 10485760 | tf_op jit(solution)/shard_map/all_gather | solution.py:882
  8.1 6.9 copy-start.37
  217.2 294.1 %reduce-scatter.3.cloned.1.call-start = ((), (), s32[]{:S(2)}) async-start(), calls=%async_computation.4 | async-start | bytes 10485760 | tf_op jit(solution)/shard_map/reduce_scatter | solution.py:879
  219.2 13.0 %copy-start.29 = (f32[2048,1]{0,1:T(1,128)}, f32[2048,1]{0,1:T(1,128)S(1)}, u32[]{:S(2)}) copy-start(f32[2048,1]{0,1:T(1,128)S(1)} %get-tuple-element.112) | copy-start | bytes 24580
  219.2 6.6 copy-start.2
  230.6 8.0 %copy-start.40 = (f32[128,2048]{1,0:T(8,128)}, f32[128,2048]{1,0:T(8,128)S(1)}, u32[]{:S(2)}) copy-start(f32[128,2048]{1,0:T(8,128)S(1)} %broadcast_dynamic-update-slice_fusion.3.lead_ref) | copy-start | bytes 3145732
  231.6 7.1 copy-start.39
  294.5 29.6 %copy-start.46 = (bf16[2048,512]{1,0:T(8,128)(2,1)S(1)}, bf16[2048,512]{1,0:T(8,128)(2,1)}, u32[]{:S(2)}) copy-start(bf16[2048,512]{1,0:T(8,128)(2,1)} %get-tuple-element.60.refs_2_) | copy-start | bytes 6291460
  366.3 359.6 %reduce-scatter.5.cloned.1.call-start = ((), (), s32[]{:S(2)}) async-start(), calls=%async_computation.5 | async-start | bytes 5242880 | tf_op jit(solution)/shard_map/reduce_scatter | solution.py:879
  725.9 6.0 copy-start.1
  725.9 6.0 copy-start.30
  726.0 6.0 copy-start.32
  726.0 6.0 copy-start.34
  730.7 11.5 %copy-start.22 = (bf16[64,6144]{1,0:T(8,128)(2,1)S(1)}, bf16[64,6144]{1,0:T(8,128)(2,1)}, u32[]{:S(2)}) copy-start(bf16[64,6144]{1,0:T(8,128)(2,1)} %get-tuple-element.82) | copy-start | bytes 2359300
  734.8 30.5 %all-to-all-start = ((f32[32,1,704]{2,1,0:T(1,128)}), f32[32,1,704]{2,1,0:T(1,128)S(1)}, u32[]{:S(2)}, u32[]{:S(2)}) async-start(f32[32,1,704]{2,1,0:T(1,128)} %reshape.193), calls=%async_computation.2 | async-start | bytes 196608 | tf_op jit(solution)/shard_map/all_to_all | solution.py:922
  742.2 5.8 copy-start.21
  753.3 6.3 copy-start.8
  753.3 6.3 copy-start.35
  753.3 6.3 copy-start.36
  759.7 5.8 copy-start.38
  759.7 5.8 copy-start.42
  759.7 5.8 copy-start.43
  (27 other events, 101.8 us)
Sparse Core Ops, SparseCore 0:
  217.3 148.8 all-gather.1
  368.6 142.6 reduce-scatter.2
  520.4 140.7 reduce-scatter.4
where the time goes:
time: 780 us; the launch traced here: 773 us
  Pallas kernels  484 us (62%)
  matrix products  158 us (20%)
  other arithmetic  63 us (8%)
  local copies, waits for them, and re-layouts  26.4 us (3%)
  waiting for transfers between devices  18.9 us (2%)
  between operations  15 us (2%)
    pallas_call x1, Pallas kernels, reduce_all(): pl.pallas_call(functools.partial(reduce_kernel, ctx, dp, seqs), in_specs=...  203 us
    pallas_call x1, Pallas kernels, gather_all(): pl.pallas_call(functools.partial(gather_kernel, ctx, dp, seqs), in_specs=...  201 us
    dot_general x6, matrix products, mm(): lax.dot_general(left, right, ((dims[:1], dims[1:]), ((), ())), preferred_...  158 us
    pallas_call x1, Pallas kernels, attend_back(): pl.pallas_call(attend_back_kernel, grid=(seqs, pairs), in_specs=[block] *...  45.8 us
    pallas_call x1, Pallas kernels, attend(): pl.pallas_call(attend_kernel, grid=(seqs, pairs), in_specs=[part(0), part...  35 us
  transfers between devices with their start and end apart: 4, of which 2 were waited for; matrix products, arithmetic and copies ran while one was open for 27% of the time, Pallas kernels for 37%

commit v1 on v0

--- a/solution.py
+++ b/solution.py
@@ -711,8 +711,7 @@
 
 def reduce_kernel(ctx, dp, seqs, *refs):
     partial, normal, attended, hidden, cot, d_qkv, d_pre = ([ref] for ref in refs[:7])
-    length = partial[0].shape[0] // seqs
-    partial = partial[0].at[pl.ds((seqs - 1) * length, length)]
+    partial = partial[0]
     refs = refs[7:]
     sum_out, qkv_out, fc1_out, out_out, fc2_out = refs[:5]
     held, downs_land, ups_land, box, x_v, turned, y_v = refs[5:12]
@@ -765,7 +764,7 @@
 
 
 def reduce_all(partial, normal, attended, hidden, cot, d_qkv, d_pre, seqs, ctx, dp):
-    length = partial.shape[0] // seqs
+    length = partial.shape[0]
     rows = length // ctx
     slab = D // dp
     copies = 2 * (ctx - 1) + 3 * (dp // 2 + dp - 2) + 6 * (ctx - 1)
@@ -818,6 +817,51 @@
     return jax.vjp(lambda vals: jax.nn.gelu(vals, approximate=True), pre)
 
 
+def finish_kernel(early, tok, cot, mix, others, last, rows, mixed, input_grad, sums):
+    step = pl.program_id(0)
+    vals = tok[...].astype(f32)
+    mixed[...] = (vals + mix[...].astype(f32) + rows[1:2, :] + rows[2:3, :]).astype(bf16)
+    normed, inv_std = normalised(vals)
+    grad = jnp.where(step < early, others[...].astype(f32), last[...])
+
+    @pl.when(step == 0)
+    def _():
+        sums[...] = jnp.zeros_like(sums)
+
+    sums[0:1, :] += jnp.sum(grad * normed, axis=0, keepdims=True)
+    sums[1:2, :] += jnp.sum(grad, axis=0, keepdims=True)
+    scaled = grad * rows[0:1, :]
+    input_grad[...] = cot[...].astype(f32) + inv_std * (
+        scaled
+        - jnp.mean(scaled, axis=-1, keepdims=True)
+        - normed * jnp.mean(scaled * normed, axis=-1, keepdims=True)
+    )
+
+
+def finish(tok, cot, mix, others, last, rows):
+    total, height = tok.shape[0], 128
+    early = others.shape[0] // height
+    block = pl.BlockSpec((height, D), lambda i: (i, 0))
+    return pl.pallas_call(
+        functools.partial(finish_kernel, early),
+        grid=(total // height,),
+        in_specs=[block] * 3
+        + [
+            pl.BlockSpec((height, D), lambda i: (jnp.minimum(i, early - 1), 0)),
+            pl.BlockSpec((height, D), lambda i: (jnp.maximum(i - early, 0), 0)),
+            pl.BlockSpec(rows.shape, lambda i: (0, 0)),
+        ],
+        out_specs=[block, block, pl.BlockSpec((8, D), lambda i: (0, 0))],
+        out_shape=[
+            jax.ShapeDtypeStruct((total, D), bf16),
+            jax.ShapeDtypeStruct((total, D), f32),
+            jax.ShapeDtypeStruct((8, D), f32),
+        ],
+        compiler_params=pltpu.CompilerParams(vmem_limit_bytes=GRANT),
+        name="finish",
+    )(tok, cot, mix, others, last, rows)
+
+
 def per_device(
     tokens,
     cotangent,
@@ -876,7 +920,7 @@
     fc1_bias = my_part(params[:, 6:10].T.reshape(FF), ff_cols)
     gain, shift = params[:, 0], params[:, 1]
     def scattered(partial):
-        return lax.psum_scatter(partial, "ctx", scatter_dimension=1, tiled=True).astype(f32)
+        return lax.psum_scatter(partial, "ctx", scatter_dimension=1, tiled=True)
 
     cot, tok_all = gate((cotangent, tok_all))
     cot_all = lax.all_gather(cot, "ctx", axis=1, tiled=True).reshape(total_rows, D)
@@ -887,49 +931,47 @@
     pre = mm(normal_low, in_w[:, 3 * head_cols :], (1, 0)) + fc1_bias
     hidden = gelu_both(pre)[0].astype(bf16)
     branch = mm(jnp.concatenate([attended, hidden], axis=1), of_w, (1, 1)).astype(bf16)
+    sum_out = jnp.sum(cotangent.astype(f32), axis=(0, 1))[None]
+    pre, hidden, branch, sum_out = gate((pre, hidden, branch, sum_out))
     pre, hidden, branch, cot_all = gate((pre, hidden, branch, cot_all))
     mix = scattered(branch.reshape(seqs, length, D))
     back = mm(cot_all, of_w[:, :head_cols], (1, 0)).astype(bf16)
     grad_hidden = mm(cot_all, of_w[:, head_cols:], (1, 0))
     d_pre = gelu_both(pre)[1](grad_hidden)[0].astype(bf16)
     d_qkv = attend_back(query, key, value, back, log_total, tables, seqs)
-    d_part = mm(jnp.concatenate([d_qkv, d_pre], axis=1), in_w, (1, 1)).astype(bf16)
-    sum_qkv, sum_pre = (jnp.sum(part, axis=0, dtype=f32) for part in (d_qkv, d_pre))
-    d_qkv, d_pre, d_part, mix, sum_qkv, sum_pre = gate(
-        (d_qkv, d_pre, d_part, mix, sum_qkv, sum_pre)
-    )
-    others = scattered(d_part[: total_rows - length].reshape(seqs - 1, length, D))
-    sum_out = jnp.sum(cotangent.astype(f32), axis=(0, 1))[None]
-    normed, inv_std = normalised(tokens.astype(f32))
-    last, grads = reduce_all(
-        d_part, normal_low, attended, hidden, cot_all, d_qkv, d_pre, seqs, ctx, dp
-    )
-    d_normal = [others[seq] for seq in range(seqs - 1)] + [last]
-
     def spread(sums, count, cols):
         whole = jnp.zeros((count, ctx * cols), f32)
         return lax.dynamic_update_slice_in_dim(whole, sums.reshape(count, cols), ctx_index * cols, 1)
 
-    sum_qkv = spread(sum_qkv, 3, head_cols)
+    sum_qkv, sum_pre = (jnp.sum(part, axis=0, dtype=f32) for part in (d_qkv, d_pre))
     sum_pre = spread(sum_pre, 1, ff_cols).reshape(4, D)
-    gain_terms = sum(jnp.sum(part * normed[seq], axis=0) for seq, part in enumerate(d_normal))[None]
-    shift_terms = sum(jnp.sum(part, axis=0) for part in d_normal)[None]
     small_terms = jnp.concatenate(
-        [gain_terms, shift_terms, sum_qkv, sum_out, sum_pre, sum_out], axis=0
-    )
+        [spread(sum_qkv, 3, head_cols), sum_out, sum_pre, sum_out], axis=0
+    )
+
+    def normal_back(first, last):
+        both = jnp.concatenate([d_qkv[first:last], d_pre[first:last]], axis=1)
+        return mm(both, in_w, (1, 1)).astype(bf16)
+
+    d_first, d_last = normal_back(0, total_rows - length), normal_back(total_rows - length, total_rows)
+    d_qkv, d_pre, d_first, d_last, small_terms = gate((d_qkv, d_pre, d_first, d_last, small_terms))
+    d_qkv, d_pre, d_first, d_last, mix = gate((d_qkv, d_pre, d_first, d_last, mix))
+    others = scattered(d_first.reshape(seqs - 1, length, D))
+    last, grads = reduce_all(
+        d_last, normal_low, attended, hidden, cot_all, d_qkv, d_pre, seqs, ctx, dp
+    )
+    mixed, input_grad, sums = finish(
+        tokens.reshape(-1, D), cotangent.reshape(-1, D), mix.reshape(-1, D), others.reshape(-1, D),
+        last, jnp.stack([gain, params[:, 5], params[:, 10]]),
+    )
+    mixed, input_grad = mixed.reshape(tokens.shape), input_grad.reshape(tokens.shape)
+    small_terms = jnp.concatenate([sums[:2], small_terms], axis=0)
     small_sent = jnp.transpose(small_terms.reshape(11, ctx * dp, own_rows), (1, 0, 2))
-    small_sent, d_normal, grads, mix = gate((small_sent, d_normal, grads, mix))
+    small_sent, grads = gate((small_sent, grads))
     small_got = lax.all_to_all(small_sent.reshape(ctx * dp, 1, 11 * own_rows), EVERY, 0, 0, tiled=True)
     small_grad = jnp.sum(small_got, axis=(0, 1)).reshape(11, own_rows).T
 
     qkv_grad, fc1_grad, out_grad, fc2_grad = (grad.astype(f32) for grad in grads)
-    mixed = (tokens.astype(f32) + mix + params[:, 5] + params[:, 10]).astype(bf16)
-    d_scaled = jnp.stack(d_normal) * gain
-    input_grad = cotangent.astype(f32) + inv_std * (
-        d_scaled
-        - jnp.mean(d_scaled, axis=-1, keepdims=True)
-        - normed * jnp.mean(d_scaled * normed, axis=-1, keepdims=True)
-    )
     qkv_new = adamw(wqkv_master, wqkv_first, wqkv_second, qkv_grad, 0.04, 0.1)
     fc1_new = adamw(fc1_master, fc1_first, fc1_second, fc1_grad, 0.04, 0.1)
     out_new = adamw(out_master, out_first, out_second, out_grad, 0.4, 0.1)

time: 780 us -> 769 us (0.986)
  other arithmetic: 63 us -> 47.9 us
  Pallas kernels: 484 us -> 498 us
    pallas_call x0 -> x1, Pallas kernels: none -> 8.73 us  [finish(): pl.pallas_call(functools.partial(finish_kernel, early), grid=(total // he...]
    unnamed x110 -> x71, local copies, waits for them, and re-layouts: 13.9 us -> 5.77 us
    dot_general x6 -> x7, matrix products: 158 us -> 159 us  [mm(): lax.dot_general(left, right, ((dims[:1], dims[1:]), ((), ())), preferred_...]
  transfers between devices with their start and end apart: 4 -> 4, of which waited for: 2 -> 2; matrix products, arithmetic and copies ran while one was open for 27% -> 27% of each run, Pallas kernels for 37% -> 38%
where the time goes in v1:
time: 769 us; the launch traced here: 762 us
  Pallas kernels  498 us (65%)
  matrix products  159 us (21%)
  other arithmetic  47.9 us (6%)
  local copies, waits for them, and re-layouts  21.1 us (3%)
  waiting for transfers between devices  15.5 us (2%)
  between operations  14.5 us (2%)
    pallas_call x1, Pallas kernels, reduce_all(): pl.pallas_call(functools.partial(reduce_kernel, ctx, dp, seqs), in_specs=...  207 us
    pallas_call x1, Pallas kernels, gather_all(): pl.pallas_call(functools.partial(gather_kernel, ctx, dp, seqs), in_specs=...  201 us
    dot_general x7, matrix products, mm(): lax.dot_general(left, right, ((dims[:1], dims[1:]), ((), ())), preferred_...  159 us
    pallas_call x1, Pallas kernels, attend_back(): pl.pallas_call(attend_back_kernel, grid=(seqs, pairs), in_specs=[block] *...  46.2 us
    pallas_call x1, Pallas kernels, attend(): pl.pallas_call(attend_kernel, grid=(seqs, pairs), in_specs=[part(0), part...  34.9 us
    sub x5, other arithmetic, adamw(): weight - step_rate * (first_hat / (jnp.sqrt(second_hat) + epsilon) + deca...  15.5 us
  transfers between devices with their start and end apart: 4, of which 2 were waited for; matrix products, arithmetic and copies ran while one was open for 27% of the time, Pallas kernels for 38%

profile of v1, /device:TPU:0, one launch (start us, length us, event | category | flops | bytes accessed | tf_op | source)
XLA Modules:
  0.0 761.7 jit_solution(10124166749845362489)
XLA Ops:
  10.5 2.7 convert_element_type.79.refs_3_
  17.5 200.9 %gather_all.1 = (bf16[2,4,256,2048]{3,2,1,0:T(8,128)(2,1)}, f32[4,8,128]{2,1,0:T(8,128)}, bf16[2048,3584]{1,0:T(8,128)(2,1)}, bf16[2048,2560]{1,0:T(8,128)(2,1)}, bf16[2048,128]{1,0:T(8,128)(2,1)}) custom-call(bf16[2,256,2048]{2,1,0:T(8,128)(2,1)} %refs_0_.1, f32[8,128]{1,0:T(8,128)} %pad.8.refs_1_, bf16[64,6144]{1,0:T(8,128)(2,1)} %convert_element_type.78.refs_2_, ...), custom_call_target="tpu_custom_call" | custom-call | tf_op jit(solution)/shard_map/gather_all/pallas_call | solution.py:407
  221.4 5.8 convert_reduce_fusion.2
  233.5 6.4 fusion.18.refs_1_
  240.0 3.2 copy-done.2
  243.2 17.5 %fusion.39.q_in.k_in.v_in = f32[2048,1536]{1,0:T(8,128)} fusion(bf16[2048,2048]{1,0:T(8,128)(2,1)S(1)} %fusion.18.refs_1_, bf16[2048,3584]{1,0:T(8,128)(2,1)} %get-tuple-element.63), kind=kOutput, calls=%fused_computation.44 | convolution fusion | flops 12884901888 | bytes 27262976 | tf_op jit(solution)/shard_map/dot_general | solution.py:41
  260.7 34.9 %attend.1 = (bf16[2048,512]{1,0:T(8,128)(2,1)}, bf16[2048,512]{1,0:T(8,128)(2,1)}, bf16[2048,512]{1,0:T(8,128)(2,1)}, bf16[2048,512]{1,0:T(8,128)(2,1)}, f32[8,2,1024]{2,1,0:T(2,128)}) custom-call(f32[2048,1536]{1,0:T(8,128)} %fusion.39.q_in.k_in.v_in, f32[2048,1536]{1,0:T(8,128)} %fusion.39.q_in.k_in.v_in, f32[2048,1536]{1,0:T(8,128)} %fusion.39.q_in.k_in.v_in, ...), custom_call_target="tpu_custom_call" | custom-call | flops 20000000000 | bytes 10000000 | tf_op jit(solution)/shard_map/attend/pallas_call | solution.py:163
  295.6 29.5 %fusion.14 = (bf16[2048,2048]{1,0:T(8,128)(2,1)}, f32[2048,2048]{1,0:T(8,128)}) fusion(f32[2048]{0:T(1024)S(1)} %dynamic_slice.7, bf16[2048,2048]{1,0:T(8,128)(2,1)} %copy-done.2, bf16[2048,3584]{1,0:T(8,128)(2,1)} %get-tuple-element.63), kind=kOutput, calls=%fused_computation.17 | convolution fusion | flops 17221812224 | bytes 41951232 | tf_op jit(solution)/shard_map/dot_general | solution.py:41
  325.1 28.3 %fusion.28 = bf16[2048,2048]{1,0:T(8,128)(2,1)} fusion(bf16[2048,2560]{1,0:T(8,128)(2,1)} %get-tuple-element.69, bf16[2048,2048]{1,0:T(8,128)(2,1)} %get-tuple-element.86.refs_3_, bf16[2048,512]{1,0:T(8,128)(2,1)S(1)} %copy-done.29), kind=kOutput, calls=%fused_computation.35 | convolution fusion | flops 21500002304 | bytes 29360128 | tf_op jit(solution)/shard_map/dot_general | solution.py:41
  354.1 13.4 %all-gather.2.cloned.1.call-done = bf16[2,1024,2048]{2,1,0:T(8,128)(2,1)} async-done(((bf16[2,256,2048]{2,1,0:T(8,128)(2,1)}), bf16[2,1024,2048]{2,1,0:T(8,128)(2,1)}) %all-gather.2.cloned.1.call-update) | async-done | bytes 8388624 | tf_op jit(solution)/shard_map/all_gather | solution.py:926
  367.5 35.8 %convert_reduce_fusion = (f32[2048]{0:T(1024)S(1)}, bf16[2048,2048]{1,0:T(8,128)(2,1)}) fusion(f32[2048,2048]{1,0:T(8,128)} %get-tuple-element.76, bf16[2048,2048]{1,0:T(8,128)(2,1)} %bitcast.80, bf16[2048,2560]{1,0:T(8,128)(2,1)} %get-tuple-element.69), kind=kOutput, calls=%fused_computation.23 | convolution fusion | flops 17272141824 | bytes 41951232 | tf_op jit(solution)/shard_map/dot_general | solution.py:41
  404.6 9.8 %convolution_convert_fusion.g_in = bf16[2048,512]{1,0:T(8,128)(2,1)} fusion(bf16[2048,2048]{1,0:T(8,128)(2,1)} %bitcast.81, bf16[2048,2560]{1,0:T(8,128)(2,1)} %get-tuple-element.69), kind=kOutput, calls=%fused_computation.51 | convolution fusion | flops 4296015872 | bytes 12582912 | tf_op jit(solution)/shard_map/dot_general | solution.py:41
  414.4 46.2 %attend_back.1.refs_5_ = bf16[2048,1536]{1,0:T(8,128)(2,1)} custom-call(bf16[2048,512]{1,0:T(8,128)(2,1)} %get-tuple-element.65.q_in, bf16[2048,512]{1,0:T(8,128)(2,1)} %get-tuple-element.66.k_in, bf16[2048,512]{1,0:T(8,128)(2,1)} %get-tuple-element.67.v_in, bf16[2048,512]{1,0:T(8,128)(2,1)} %convolution_convert_fusion.g_in, ...), custom_call_target="tpu_custom_call" | custom-call | flops 30000001024 | bytes 10000000 | tf_op jit(solution)/shard_map/attend_back/pallas_call | solution.py:181
  460.6 3.8 convert_reduce_fusion.1
  465.1 3.2 fusion.82
  468.4 3.9 fusion.81
  472.3 19.0 %fusion.44 = bf16[1024,2048]{1,0:T(8,128)(2,1)} fusion(bf16[2048,3584]{1,0:T(8,128)(2,1)} %get-tuple-element.63, bf16[1024,2048]{1,0:T(8,128)(2,1)S(1)} %get-tuple-element.119, bf16[1024,1536]{1,0:T(8,128)(2,1)S(1)} %get-tuple-element.121), kind=kOutput, calls=%fused_computation.48 | convolution fusion | flops 15049162752 | bytes 26214400 | tf_op jit(solution)/shard_map/dot_general | solution.py:41
  491.3 19.2 %fusion.41.refs_0_ = bf16[1024,2048]{1,0:T(8,128)(2,1)} fusion(bf16[2048,3584]{1,0:T(8,128)(2,1)} %get-tuple-element.63, bf16[1024,2048]{1,0:T(8,128)(2,1)S(1)} %get-tuple-element.118, bf16[1024,1536]{1,0:T(8,128)(2,1)S(1)} %get-tuple-element.120), kind=kOutput, calls=%fused_computation.47 | convolution fusion | flops 15049162752 | bytes 26214400 | tf_op jit(solution)/shard_map/dot_general | solution.py:41
  512.5 207.0 %reduce_all.1 = (f32[256,2048]{1,0:T(8,128)}, bf16[64,6144]{1,0:T(8,128)(2,1)}, bf16[64,8192]{1,0:T(8,128)(2,1)}, bf16[64,2048]{1,0:T(8,128)(2,1)}, bf16[64,8192]{1,0:T(8,128)(2,1)}) custom-call(bf16[1024,2048]{1,0:T(8,128)(2,1)} %fusion.41.refs_0_, bf16[2048,2048]{1,0:T(8,128)(2,1)} %copy-done.2, bf16[2048,512]{1,0:T(8,128)(2,1)} %get-tuple-element.68.refs_2_, ...), custom_call_target="tpu_custom_call" | custom-call | flops 149999992832 | bytes 100000000 | tf_op jit(solution)/shard_map/reduce_all/pallas_call | solution.py:775
  719.6 8.7 %finish.1 = (bf16[512,2048]{1,0:T(8,128)(2,1)}, f32[512,2048]{1,0:T(8,128)}, f32[8,2048]{1,0:T(8,128)}) custom-call(bf16[512,2048]{1,0:T(8,128)(2,1)} %bitcast.63, bf16[512,2048]{1,0:T(8,128)(2,1)} %bitcast.61, bf16[512,2048]{1,0:T(8,128)(2,1)} %bitcast.65, bf16[256,2048]{1,0:T(8,128)(2,1)} %bitcast.66, f32[256,2048]{1,0:T(8,128)} %get-tuple-element.89.last, ...), custom_call_target="tpu_custom_call" | custom-call | tf_op jit(solution)/shard_map/finish/pallas_call | solution.py:845
  732.0 5.8 all-to-all-start
  737.8 5.7 multiply_subtract_fusion.2
  743.5 3.9 multiply_subtract_fusion.1
  748.9 3.8 multiply_subtract_fusion
  (128 shorter events, 28.8 us)
Async XLA Ops:
  7.2 8.9 %copy-start.21 = (f32[64,11]{0,1:T(8,128)S(1)}, f32[64,11]{0,1:T(8,128)}, u32[]{:S(2)}) copy-start(f32[64,11]{0,1:T(8,128)} %param.25) | copy-start | bytes 8452
  7.2 360.2 %all-gather.2.cloned.1.call-start = ((), (), s32[]{:S(2)}) async-start(), calls=%async_computation.3 | async-start | bytes 10485760 | tf_op jit(solution)/shard_map/all_gather | solution.py:926
  7.9 7.1 copy-start.4
  13.1 207.3 %copy-start.1 = (bf16[2,256,2048]{2,1,0:T(8,128)(2,1)S(1)}, bf16[2,256,2048]{2,1,0:T(8,128)(2,1)}, u32[]{:S(2)}) copy-start(bf16[2,256,2048]{2,1,0:T(8,128)(2,1)} %param.19) | copy-start | bytes 6291460
  218.4 294.1 %reduce-scatter.3.cloned.1.call-start = ((), (), s32[]{:S(2)}) async-start(), calls=%async_computation.4 | async-start | bytes 10485760 | tf_op jit(solution)/shard_map/reduce_scatter | solution.py:923
  219.7 7.5 copy-start
  232.0 8.0 %copy-start.24 = (f32[128,2048]{1,0:T(8,128)}, f32[128,2048]{1,0:T(8,128)S(1)}, u32[]{:S(2)}) copy-start(f32[128,2048]{1,0:T(8,128)S(1)} %broadcast_dynamic-update-slice_fusion.3.lead_ref) | copy-start | bytes 3145732
  232.9 7.1 copy-start.23
  295.6 29.5 %copy-start.29 = (bf16[2048,512]{1,0:T(8,128)(2,1)S(1)}, bf16[2048,512]{1,0:T(8,128)(2,1)}, u32[]{:S(2)}) copy-start(bf16[2048,512]{1,0:T(8,128)(2,1)} %get-tuple-element.68.refs_2_) | copy-start | bytes 6291460
  325.1 28.3 %copy-start.18 = (f32[1,2048]{1,0:T(1,128)S(1)}, f32[1,2048]{1,0:T(1,128)}, u32[]{:S(2)}) copy-start(f32[1,2048]{1,0:T(1,128)} %get-tuple-element.122) | copy-start | bytes 24580
  325.1 28.3 %copy-start.19 = (f32[1,2048]{1,0:T(1,128)S(1)}, f32[1,2048]{1,0:T(1,128)}, u32[]{:S(2)}) copy-start(f32[1,2048]{1,0:T(1,128)} %get-tuple-element.123) | copy-start | bytes 24580
  325.1 28.3 %copy-start.20 = (f32[1,2048]{1,0:T(1,128)S(1)}, f32[1,2048]{1,0:T(1,128)}, u32[]{:S(2)}) copy-start(f32[1,2048]{1,0:T(1,128)} %get-tuple-element.124) | copy-start | bytes 24580
  367.5 352.1 %reduce-scatter.5.cloned.1.call-start = ((), (), s32[]{:S(2)}) async-start(), calls=%async_computation.5 | async-start | bytes 5242880 | tf_op jit(solution)/shard_map/reduce_scatter | solution.py:923
  719.5 9.8 %copy-start.13 = (f32[9,2048]{1,0:T(8,128)S(1)}, f32[9,2048]{1,0:T(8,128)}, u32[]{:S(2)}) copy-start(f32[9,2048]{1,0:T(8,128)} %pad_maximum_fusion) | copy-start | bytes 221188
  728.3 15.2 %copy-start.3 = (f32[64,8192]{1,0:T(8,128)S(1)}, f32[64,8192]{1,0:T(8,128)}, u32[]{:S(2)}) copy-start(f32[64,8192]{1,0:T(8,128)} %param.22) | copy-start | bytes 6291460
  728.3 15.2 %copy-start.12 = (bf16[64,8192]{1,0:T(8,128)(2,1)S(1)}, bf16[64,8192]{1,0:T(8,128)(2,1)}, u32[]{:S(2)}) copy-start(bf16[64,8192]{1,0:T(8,128)(2,1)} %get-tuple-element.99) | copy-start | bytes 3145732
  732.0 22.2 %all-to-all-start = ((f32[32,1,704]{2,1,0:T(1,128)}), f32[32,1,704]{2,1,0:T(1,128)S(1)}, u32[]{:S(2)}, u32[]{:S(2)}) async-start(f32[32,1,704]{2,1,0:T(1,128)} %reshape.151), calls=%async_computation.2 | async-start | bytes 196608 | tf_op jit(solution)/shard_map/all_to_all | solution.py:971
  737.8 5.7 copy-start.7
  737.8 5.7 copy-start.8
  743.5 5.1 copy-start.10
  743.5 5.3 copy-start.11
  748.9 5.4 copy-start.22
  748.9 5.4 copy-start.26
  748.9 5.4 copy-start.27
  (10 other events, 33.9 us)
Sparse Core Ops, SparseCore 0:
  218.5 148.8 all-gather.1
  369.8 142.6 reduce-scatter.2
  515.4 142.8 reduce-scatter.4

commit v2 on v1

--- a/solution.py
+++ b/solution.py
@@ -207,9 +207,6 @@
 
 
 def run_chains(chains):
-    chains = [chain for chain in chains]
-    for chain in chains:
-        next(chain)
     while chains:
         left = []
         for chain in chains:
@@ -374,18 +371,38 @@
     return [first, [(out, head_cols, 0, 0), (fc2, ff_cols, 0, head_cols)], [(small, LANES, None, 0)]]
 
 
+def rounded_into(target, source):
+    @pl.loop(0, source.shape[0] // 16)
+    def _(index):
+        at = pl.ds(pl.multiple_of(index * 16, 16), 16)
+        target[at, :] = source[at, :].astype(bf16)
+
+
 def gather_kernel(ctx, dp, seqs, *refs):
-    tokens, places, blocks = refs[0], refs[1], refs[2:7]
+    tokens, places, masters, small = refs[0], refs[1], refs[2:6], refs[6]
     tok_out, place_out, outs = refs[7], refs[8], refs[9:12]
-    send, recv, own_sems, tok_sems = refs[12:]
+    wide, low = refs[12:16], refs[16:20]
+    send, recv, own_sems, tok_sems, load_sems = refs[20:]
     here = lax.axis_index("ctx")
     sems = Sems(send, recv)
+    loads = [
+        pltpu.make_async_copy(masters[index], wide[index], load_sems.at[index]) for index in range(4)
+    ]
+    for load in loads:
+        load.start()
     greet(ctx, dp)
-    chains = [line_chain(places, place_out, sems, ctx)]
-    for group, cuts in enumerate(cuts_of(blocks, ctx)):
-        chains.append(weight_chain(cuts, outs[group], sems, own_sems.at[group], ctx, dp))
-        if group < seqs:
-            chains.append(line_chain(tokens.at[group], tok_out.at[group], sems, ctx))
+    weights = []
+    for group, cuts in enumerate(cuts_of([*low, small], ctx)):
+        for index in ((0, 1), (2, 3), ())[group]:
+            loads[index].wait()
+            rounded_into(low[index], wide[index])
+        weights.append(weight_chain(cuts, outs[group], sems, own_sems.at[group], ctx, dp))
+        next(weights[group])
+    place = line_chain(places, place_out, sems, ctx)
+    lines = [line_chain(tokens.at[seq], tok_out.at[seq], sems, ctx) for seq in range(seqs)]
+    for chain in (place, *lines):
+        next(chain)
+    chains = [place, weights[0], lines[0], weights[1], *lines[1:], weights[2]]
     local = [
         pltpu.make_async_copy(tokens.at[seq], tok_out.at[seq, here], tok_sems.at[seq])
         for seq in range(seqs)
@@ -416,12 +433,17 @@
             jax.ShapeDtypeStruct((rows, LANES), bf16),
         ],
         scratch_shapes=[
+            *[pltpu.VMEM(block.shape, f32) for block in blocks[:4]],
+            *[pltpu.VMEM(block.shape, bf16) for block in blocks[:4]],
             pltpu.SemaphoreType.DMA((copies,)),
             pltpu.SemaphoreType.DMA((copies,)),
             pltpu.SemaphoreType.DMA((3, 4)),
             pltpu.SemaphoreType.DMA((seqs + 1,)),
+            pltpu.SemaphoreType.DMA((4,)),
         ],
-        compiler_params=pltpu.CompilerParams(collective_id=1, has_side_effects=True),
+        compiler_params=pltpu.CompilerParams(
+            collective_id=1, has_side_effects=True, vmem_limit_bytes=GRANT
+        ),
         name="gather_all",
     )(tokens, places, *blocks)
     return outs[0], outs[1], outs[2:]
@@ -892,8 +914,7 @@
 
     gate = lax.optimization_barrier
     small_low = jnp.pad(small_master.astype(bf16), ((0, 0), (0, LANES - small_master.shape[1])))
-    blocks = [wqkv_master, fc1_master, out_master, fc2_master]
-    blocks = [block.astype(bf16) for block in blocks] + [small_low]
+    blocks = [wqkv_master, fc1_master, out_master, fc2_master, small_low]
     places = jnp.pad(positions.astype(f32).reshape(-1, LANES), ((0, 8 - seqs * span // LANES), (0, 0)))
     tok_all, place, (in_w, of_w, small_all) = gather_all(tokens, places, blocks, ctx, dp)
     qkv_w, fc1_w = in_w[:, : 3 * head_cols], in_w[:, 3 * head_cols :]

time: 769 us -> 761 us (0.990)
  other arithmetic: 47.9 us -> 40.2 us
    convert_element_type x4 -> x0, other arithmetic: 8.17 us -> none  [per_device(): blocks = [block.astype(bf16) for block in blocks] + [small_low]]
  transfers between devices with their start and end apart: 4 -> 4, of which waited for: 2 -> 2; matrix products, arithmetic and copies ran while one was open for 27% -> 28% of each run, Pallas kernels for 38% -> 38%
where the time goes in v2:
time: 761 us; the launch traced here: 754 us
  Pallas kernels  493 us (65%)
  matrix products  159 us (21%)
  other arithmetic  40.2 us (5%)
  local copies, waits for them, and re-layouts  21.1 us (3%)
  waiting for transfers between devices  20 us (3%)
  between operations  14.5 us (2%)
    pallas_call x1, Pallas kernels, reduce_all(): pl.pallas_call(functools.partial(reduce_kernel, ctx, dp, seqs), in_specs=...  207 us
    pallas_call x1, Pallas kernels, gather_all(): pl.pallas_call(functools.partial(gather_kernel, ctx, dp, seqs), in_specs=...  196 us
    dot_general x7, matrix products, mm(): lax.dot_general(left, right, ((dims[:1], dims[1:]), ((), ())), preferred_...  159 us
    pallas_call x1, Pallas kernels, attend_back(): pl.pallas_call(attend_back_kernel, grid=(seqs, pairs), in_specs=[block] *...  46.2 us
    pallas_call x1, Pallas kernels, attend(): pl.pallas_call(attend_kernel, grid=(seqs, pairs), in_specs=[part(0), part...  35 us
    all_gather x1, waiting for transfers between devices, per_device(): lax.all_gather(cot, 'ctx', axis=1, tiled=True).reshape(total_rows, D)  17.9 us
    sub x5, other arithmetic, adamw(): weight - step_rate * (first_hat / (jnp.sqrt(second_hat) + epsilon) + deca...  15.5 us
  transfers between devices with their start and end apart: 4, of which 2 were waited for; matrix products, arithmetic and copies ran while one was open for 28% of the time, Pallas kernels for 38%

profile of v2, /device:TPU:0, one launch (start us, length us, event | category | flops | bytes accessed | tf_op | source)
XLA Modules:
  0.0 753.9 jit_solution(1950729005053232600)
XLA Ops:
  10.1 196.2 %gather_all.1 = (bf16[2,4,256,2048]{3,2,1,0:T(8,128)(2,1)}, f32[4,8,128]{2,1,0:T(8,128)}, bf16[2048,3584]{1,0:T(8,128)(2,1)}, bf16[2048,2560]{1,0:T(8,128)(2,1)}, bf16[2048,128]{1,0:T(8,128)(2,1)}) custom-call(bf16[2,256,2048]{2,1,0:T(8,128)(2,1)} %refs_0_.1, f32[8,128]{1,0:T(8,128)} %pad.8.refs_1_, f32[64,6144]{1,0:T(8,128)} %refs_2_.1, ...), custom_call_target="tpu_custom_call" | custom-call | tf_op jit(solution)/shard_map/gather_all/pallas_call | solution.py:424
  209.4 5.2 convert_reduce_fusion.2
  214.7 2.3 multiply_reduce_fusion
  221.0 6.6 fusion.18.refs_1_
  227.6 3.2 copy-done.2
  230.8 17.5 %fusion.39.q_in.k_in.v_in = f32[2048,1536]{1,0:T(8,128)} fusion(bf16[2048,2048]{1,0:T(8,128)(2,1)S(1)} %fusion.18.refs_1_, bf16[2048,3584]{1,0:T(8,128)(2,1)} %get-tuple-element.63), kind=kOutput, calls=%fused_computation.44 | convolution fusion | flops 12884901888 | bytes 27262976 | tf_op jit(solution)/shard_map/dot_general | solution.py:41
  248.3 35.0 %attend.1 = (bf16[2048,512]{1,0:T(8,128)(2,1)}, bf16[2048,512]{1,0:T(8,128)(2,1)}, bf16[2048,512]{1,0:T(8,128)(2,1)}, bf16[2048,512]{1,0:T(8,128)(2,1)}, f32[8,2,1024]{2,1,0:T(2,128)}) custom-call(f32[2048,1536]{1,0:T(8,128)} %fusion.39.q_in.k_in.v_in, f32[2048,1536]{1,0:T(8,128)} %fusion.39.q_in.k_in.v_in, f32[2048,1536]{1,0:T(8,128)} %fusion.39.q_in.k_in.v_in, ...), custom_call_target="tpu_custom_call" | custom-call | flops 20000000000 | bytes 10000000 | tf_op jit(solution)/shard_map/attend/pallas_call | solution.py:163
  283.3 29.6 %fusion.14 = (bf16[2048,2048]{1,0:T(8,128)(2,1)}, f32[2048,2048]{1,0:T(8,128)}) fusion(f32[2048]{0:T(1024)S(1)} %dynamic_slice.7, bf16[2048,2048]{1,0:T(8,128)(2,1)} %copy-done.2, bf16[2048,3584]{1,0:T(8,128)(2,1)} %get-tuple-element.63), kind=kOutput, calls=%fused_computation.17 | convolution fusion | flops 17221812224 | bytes 41951232 | tf_op jit(solution)/shard_map/dot_general | solution.py:41
  312.9 28.3 %fusion.28 = bf16[2048,2048]{1,0:T(8,128)(2,1)} fusion(bf16[2048,2560]{1,0:T(8,128)(2,1)} %get-tuple-element.69, bf16[2048,2048]{1,0:T(8,128)(2,1)} %get-tuple-element.86.refs_3_, bf16[2048,512]{1,0:T(8,128)(2,1)S(1)} %copy-done.27), kind=kOutput, calls=%fused_computation.35 | convolution fusion | flops 21500002304 | bytes 29360128 | tf_op jit(solution)/shard_map/dot_general | solution.py:41
  341.8 17.9 %all-gather.2.cloned.1.call-done = bf16[2,1024,2048]{2,1,0:T(8,128)(2,1)} async-done(((bf16[2,256,2048]{2,1,0:T(8,128)(2,1)}), bf16[2,1024,2048]{2,1,0:T(8,128)(2,1)}) %all-gather.2.cloned.1.call-update) | async-done | bytes 8388624 | tf_op jit(solution)/shard_map/all_gather | solution.py:947
  359.7 35.8 %convert_reduce_fusion = (f32[2048]{0:T(1024)S(1)}, bf16[2048,2048]{1,0:T(8,128)(2,1)}) fusion(f32[2048,2048]{1,0:T(8,128)} %get-tuple-element.76, bf16[2048,2048]{1,0:T(8,128)(2,1)} %bitcast.80, bf16[2048,2560]{1,0:T(8,128)(2,1)} %get-tuple-element.69), kind=kOutput, calls=%fused_computation.23 | convolution fusion | flops 17272141824 | bytes 41951232 | tf_op jit(solution)/shard_map/dot_general | solution.py:41
  396.8 9.8 %convolution_convert_fusion.g_in = bf16[2048,512]{1,0:T(8,128)(2,1)} fusion(bf16[2048,2048]{1,0:T(8,128)(2,1)} %bitcast.81, bf16[2048,2560]{1,0:T(8,128)(2,1)} %get-tuple-element.69), kind=kOutput, calls=%fused_computation.51 | convolution fusion | flops 4296015872 | bytes 12582912 | tf_op jit(solution)/shard_map/dot_general | solution.py:41
  406.7 46.2 %attend_back.1.refs_5_ = bf16[2048,1536]{1,0:T(8,128)(2,1)} custom-call(bf16[2048,512]{1,0:T(8,128)(2,1)} %get-tuple-element.65.q_in, bf16[2048,512]{1,0:T(8,128)(2,1)} %get-tuple-element.66.k_in, bf16[2048,512]{1,0:T(8,128)(2,1)} %get-tuple-element.67.v_in, bf16[2048,512]{1,0:T(8,128)(2,1)} %convolution_convert_fusion.g_in, ...), custom_call_target="tpu_custom_call" | custom-call | flops 30000001024 | bytes 10000000 | tf_op jit(solution)/shard_map/attend_back/pallas_call | solution.py:181
  452.8 3.8 convert_reduce_fusion.1
  457.4 3.2 fusion.82
  460.6 3.9 fusion.81
  464.5 19.0 %fusion.44 = bf16[1024,2048]{1,0:T(8,128)(2,1)} fusion(bf16[2048,3584]{1,0:T(8,128)(2,1)} %get-tuple-element.63, bf16[1024,2048]{1,0:T(8,128)(2,1)S(1)} %get-tuple-element.119, bf16[1024,1536]{1,0:T(8,128)(2,1)S(1)} %get-tuple-element.121), kind=kOutput, calls=%fused_computation.48 | convolution fusion | flops 15049162752 | bytes 26214400 | tf_op jit(solution)/shard_map/dot_general | solution.py:41
  483.5 19.2 %fusion.41.refs_0_ = bf16[1024,2048]{1,0:T(8,128)(2,1)} fusion(bf16[2048,3584]{1,0:T(8,128)(2,1)} %get-tuple-element.63, bf16[1024,2048]{1,0:T(8,128)(2,1)S(1)} %get-tuple-element.118, bf16[1024,1536]{1,0:T(8,128)(2,1)S(1)} %get-tuple-element.120), kind=kOutput, calls=%fused_computation.47 | convolution fusion | flops 15049162752 | bytes 26214400 | tf_op jit(solution)/shard_map/dot_general | solution.py:41
  504.8 207.0 %reduce_all.1 = (f32[256,2048]{1,0:T(8,128)}, bf16[64,6144]{1,0:T(8,128)(2,1)}, bf16[64,8192]{1,0:T(8,128)(2,1)}, bf16[64,2048]{1,0:T(8,128)(2,1)}, bf16[64,8192]{1,0:T(8,128)(2,1)}) custom-call(bf16[1024,2048]{1,0:T(8,128)(2,1)} %fusion.41.refs_0_, bf16[2048,2048]{1,0:T(8,128)(2,1)} %copy-done.2, bf16[2048,512]{1,0:T(8,128)(2,1)} %get-tuple-element.68.refs_2_, ...), custom_call_target="tpu_custom_call" | custom-call | flops 149999992832 | bytes 100000000 | tf_op jit(solution)/shard_map/reduce_all/pallas_call | solution.py:797
  711.8 8.7 %finish.1 = (bf16[512,2048]{1,0:T(8,128)(2,1)}, f32[512,2048]{1,0:T(8,128)}, f32[8,2048]{1,0:T(8,128)}) custom-call(bf16[512,2048]{1,0:T(8,128)(2,1)} %bitcast.63, bf16[512,2048]{1,0:T(8,128)(2,1)} %bitcast.61, bf16[512,2048]{1,0:T(8,128)(2,1)} %bitcast.65, bf16[256,2048]{1,0:T(8,128)(2,1)} %bitcast.66, f32[256,2048]{1,0:T(8,128)} %get-tuple-element.89.last, ...), custom_call_target="tpu_custom_call" | custom-call | tf_op jit(solution)/shard_map/finish/pallas_call | solution.py:867
  724.2 5.8 all-to-all-start
  730.0 5.7 multiply_subtract_fusion.2
  735.8 3.9 multiply_subtract_fusion.1
  741.1 3.8 multiply_subtract_fusion
  (120 shorter events, 21.7 us)
Async XLA Ops:
  7.2 201.2 %copy-start.1 = (bf16[2,256,2048]{2,1,0:T(8,128)(2,1)S(1)}, bf16[2,256,2048]{2,1,0:T(8,128)(2,1)}, u32[]{:S(2)}) copy-start(bf16[2,256,2048]{2,1,0:T(8,128)(2,1)} %param.19) | copy-start | bytes 6291460
  7.2 352.5 %all-gather.2.cloned.1.call-start = ((), (), s32[]{:S(2)}) async-start(), calls=%async_computation.3 | async-start | bytes 10485760 | tf_op jit(solution)/shard_map/all_gather | solution.py:947
  206.4 298.4 %reduce-scatter.3.cloned.1.call-start = ((), (), s32[]{:S(2)}) async-start(), calls=%async_computation.4 | async-start | bytes 10485760 | tf_op jit(solution)/shard_map/reduce_scatter | solution.py:944
  207.7 7.0 copy-start
  219.4 8.1 %copy-start.22 = (f32[128,2048]{1,0:T(8,128)}, f32[128,2048]{1,0:T(8,128)S(1)}, u32[]{:S(2)}) copy-start(f32[128,2048]{1,0:T(8,128)S(1)} %broadcast_dynamic-update-slice_fusion.3.lead_ref) | copy-start | bytes 3145732
  220.3 7.2 copy-start.21
  283.3 29.6 %copy-start.27 = (bf16[2048,512]{1,0:T(8,128)(2,1)S(1)}, bf16[2048,512]{1,0:T(8,128)(2,1)}, u32[]{:S(2)}) copy-start(bf16[2048,512]{1,0:T(8,128)(2,1)} %get-tuple-element.68.refs_2_) | copy-start | bytes 6291460
  312.8 28.3 %copy-start.17 = (f32[1,2048]{1,0:T(1,128)S(1)}, f32[1,2048]{1,0:T(1,128)}, u32[]{:S(2)}) copy-start(f32[1,2048]{1,0:T(1,128)} %get-tuple-element.122) | copy-start | bytes 24580
  312.9 28.3 %copy-start.18 = (f32[1,2048]{1,0:T(1,128)S(1)}, f32[1,2048]{1,0:T(1,128)}, u32[]{:S(2)}) copy-start(f32[1,2048]{1,0:T(1,128)} %get-tuple-element.123) | copy-start | bytes 24580
  312.9 28.3 %copy-start.19 = (f32[1,2048]{1,0:T(1,128)S(1)}, f32[1,2048]{1,0:T(1,128)}, u32[]{:S(2)}) copy-start(f32[1,2048]{1,0:T(1,128)} %get-tuple-element.124) | copy-start | bytes 24580
  359.7 352.1 %reduce-scatter.5.cloned.1.call-start = ((), (), s32[]{:S(2)}) async-start(), calls=%async_computation.5 | async-start | bytes 5242880 | tf_op jit(solution)/shard_map/reduce_scatter | solution.py:944
  711.8 9.8 %copy-start.12 = (f32[9,2048]{1,0:T(8,128)S(1)}, f32[9,2048]{1,0:T(8,128)}, u32[]{:S(2)}) copy-start(f32[9,2048]{1,0:T(8,128)} %pad_maximum_fusion) | copy-start | bytes 221188
  720.5 15.2 %copy-start.3 = (f32[64,8192]{1,0:T(8,128)S(1)}, f32[64,8192]{1,0:T(8,128)}, u32[]{:S(2)}) copy-start(f32[64,8192]{1,0:T(8,128)} %refs_3_.1) | copy-start | bytes 6291460
  720.6 15.2 %copy-start.11 = (bf16[64,8192]{1,0:T(8,128)(2,1)S(1)}, bf16[64,8192]{1,0:T(8,128)(2,1)}, u32[]{:S(2)}) copy-start(bf16[64,8192]{1,0:T(8,128)(2,1)} %get-tuple-element.99) | copy-start | bytes 3145732
  724.2 22.2 %all-to-all-start = ((f32[32,1,704]{2,1,0:T(1,128)}), f32[32,1,704]{2,1,0:T(1,128)S(1)}, u32[]{:S(2)}, u32[]{:S(2)}) async-start(f32[32,1,704]{2,1,0:T(1,128)} %reshape.151), calls=%async_computation.2 | async-start | bytes 196608 | tf_op jit(solution)/shard_map/all_to_all | solution.py:992
  730.0 5.7 copy-start.5
  730.0 5.7 copy-start.6
  735.7 4.0 copy-start.4
  735.7 4.0 copy-start.7
  735.8 5.1 copy-start.8
  735.8 5.3 copy-start.10
  741.1 5.4 copy-start.20
  741.1 5.4 copy-start.24
  741.1 5.4 copy-start.25
  (8 other events, 26.0 us)
Sparse Core Ops, SparseCore 0:
  206.5 153.1 all-gather.1
  362.0 142.6 reduce-scatter.2
  507.6 142.8 reduce-scatter.4
